TPU v7x, 512 devices: a whole 4x4x16 slice. The times are simulated.
512 devices in a mesh: frames: 64 (over y, z), tok: 2 (over core), dp: 4 (over x).
Axes of the slice: x: 4, y: 4, z: 16, core: 2. Of those that a mesh axis runs over, the one named last changes fastest.
Arguments:
- frame_input: bfloat16 [32768, 1024], P(('dp', 'frames'), 'tok'), parts along dimension 0, may hold values from -6 to 6
- state_write: bfloat16 [32768, 128], P(('dp', 'frames')), parts along dimension 0, may hold values from -0.3125 to 0.3125
- state_read: bfloat16 [32768, 128], P(('dp', 'frames')), parts along dimension 0, may hold values from -0.5 to 0.5
- log_decay: float32 [2, 16, 32768], P(None, 'tok', ('dp', 'frames')), parts along dimension 2, may hold values from -2 to 0, as said below
- skip_gain: float32 [16], P('tok'), may hold values from 0.5 to 1.5
- key_weight: bfloat16 [1024, 1280], P(None, 'tok'), may hold values from -0.1875 to 0.1875
- value_weight: bfloat16 [1024, 1280], P(None, 'tok'), may hold values from -0.1875 to 0.1875
- queries: bfloat16 [65536, 1280], P(('dp', 'frames'), 'tok'), parts along dimension 0, may hold values from -160 to 160
- span_start: int32 [1024], P(('dp', 'frames')), parts along dimension 0, may hold values from 0 to 8128, as said below
- span_len: int32 [1024], P(('dp', 'frames')), parts along dimension 0, may hold values from 64 to 128, as said below
Outputs:
- encoded: bfloat16 [32768, 1024], P(('dp', 'frames'), 'tok'), parts along dimension 0
- attended: bfloat16 [65536, 1280], P(('dp', 'frames'), 'tok'), parts along dimension 0
There are 4 independent parts, one for each index of `dp`. A program takes and returns all parts, laid end to end along the dimension named above; an argument that names none is the same for every part. Nothing has to cross between parts.
Inputs may be any that keep to these rules, and one draw needn't show every extreme that they name: `log_decay`: Nonpositive. `span_start`: A multiple of 64. The span of group g lies within frames g // 4 * 128 - 64 to (g // 4 + 1) * 128 + 63 and within the recording. The first group's span starts at frame 0; the last group's span is the last 64 frames. `span_len`: A multiple of 64.
All inputs are finite; a program needn't handle non-finite values.
Results may differ from a plain program's by a relative error of at most 0.022.
Values may be sent and summed in bfloat16 or wider, within the bound.
A program may use at most 128 MiB of HBM per device.

v0:
```python
import jax
import jax.numpy as jnp
from jax import lax
from jax.sharding import PartitionSpec as P

DHD = 64


def entering(part, axis, combine, identity, reverse):
    count = lax.axis_size(axis)
    place = lax.axis_index(axis)
    ahead = count - 1 - place if reverse else place
    gathered = jax.tree.map(lambda a: lax.all_gather(a, axis), part)
    state = jax.tree.map(lambda a, e: jnp.zeros_like(a) + jnp.asarray(e, a.dtype), part, identity)

    def one(step, state):
        source = count - 1 - step if reverse else step
        return combine(
            state, jax.tree.map(lambda a: lax.dynamic_index_in_dim(a, source, 0, False), gathered)
        )

    return lax.fori_loop(0, ahead, one, state)


def with_halo(cells, sides, width):
    for axis, dim in sides:
        count = lax.axis_size(axis)
        ends = count - 1
        head = lax.slice_in_dim(cells, 0, width, axis=dim)
        tail = lax.slice_in_dim(cells, cells.shape[dim] - width, cells.shape[dim], axis=dim)
        cells = jnp.concatenate(
            [
                lax.ppermute(tail, axis, [(i, (i + 1) % count) for i in range(ends)]),
                cells,
                lax.ppermute(head, axis, [((i + 1) % count, i) for i in range(ends)]),
            ],
            axis=dim,
        )
    return cells


def block_terms(x_block, b_block, gram_matrix, rate_block):
    block_size = rate_block.shape[1]
    cumulative = jnp.cumsum(rate_block, axis=1)
    spread = cumulative[:, :, None] - cumulative[:, None, :]
    row_ids = jnp.arange(block_size)
    causal = (row_ids[:, None] >= row_ids[None, :])[None]
    weights = jnp.where(causal, jnp.exp(jnp.where(causal, spread, 0.0)), 0.0) * gram_matrix[None]
    weights = weights.astype(jnp.bfloat16)
    intra_part = jnp.einsum("hts,shp->thp", weights, x_block, preferred_element_type=jnp.float32)
    to_end = jnp.exp(cumulative[:, -1:] - cumulative)
    scaled = (x_block.astype(jnp.float32) * to_end.T[:, :, None]).astype(jnp.bfloat16)
    local_state = jnp.einsum("fhp,fn->hpn", scaled, b_block, preferred_element_type=jnp.float32)
    return (intra_part, local_state, jnp.exp(cumulative[:, -1]), cumulative)


def carried_output(c_block, state, cumulative):
    reading = jnp.einsum(
        "fn,hpn->fhp", c_block, state.astype(jnp.bfloat16), preferred_element_type=jnp.float32
    )
    return jnp.exp(cumulative).T[:, :, None] * reading


def chain_combine(earlier, later):
    return (earlier[0] * later[0], later[0][:, None, None] * earlier[1] + later[1])


def local(
    frame_input,
    state_write,
    state_read,
    log_decay,
    skip_gain,
    key_weight,
    value_weight,
    queries,
    span_start,
    span_len,
):
    frame_count, width_local = frame_input.shape
    heads_local = log_decay.shape[1]
    head_width = width_local // heads_local
    x_heads = frame_input.reshape(frame_count, heads_local, head_width)
    gram_matrix = jnp.einsum(
        "tn,sn->ts", state_read, state_write, preferred_element_type=jnp.float32
    )
    forward_part, forward_state, forward_total, forward_cum = block_terms(
        x_heads, state_write, gram_matrix, log_decay[0]
    )
    x_reversed = x_heads[::-1]
    b_reversed = state_write[::-1]
    c_reversed = state_read[::-1]
    backward_part, backward_state, backward_total, backward_cum = block_terms(
        x_reversed, b_reversed, gram_matrix[::-1, ::-1], log_decay[1][:, ::-1]
    )
    identity = (jnp.ones((heads_local,), jnp.float32), jnp.zeros_like(forward_state))
    entering_fwd = entering(
        (forward_total, forward_state), "frames", chain_combine, identity, False
    )
    entering_bwd = entering(
        (backward_total, backward_state), "frames", chain_combine, identity, True
    )
    forward_out = forward_part + carried_output(state_read, entering_fwd[1], forward_cum)
    backward_out = (backward_part + carried_output(c_reversed, entering_bwd[1], backward_cum))[::-1]
    combined = forward_out + backward_out + skip_gain[None, :, None] * x_heads.astype(jnp.float32)
    encoded = combined.reshape(frame_count, width_local).astype(jnp.bfloat16)
    features = lax.all_gather(encoded, "tok", axis=1, tiled=True)
    rim_width = frame_count // 2
    widened = with_halo(features, (("frames", 0),), rim_width)
    keys = jnp.dot(widened, key_weight, preferred_element_type=jnp.float32).astype(jnp.bfloat16)
    values = jnp.dot(widened, value_weight, preferred_element_type=jnp.float32).astype(jnp.bfloat16)
    token_count, query_width = queries.shape
    dec_heads = query_width // DHD
    window_rows = keys.shape[0]
    per_group = token_count // span_start.shape[0]
    first_frame = lax.axis_index("frames") * frame_count - rim_width
    positions = first_frame + jnp.arange(window_rows, dtype=jnp.int32)
    token_starts = jnp.repeat(span_start, per_group, total_repeat_length=token_count)
    token_ends = token_starts + jnp.repeat(span_len, per_group, total_repeat_length=token_count)
    allowed = (positions[None, :] >= token_starts[:, None]) & (
        positions[None, :] < token_ends[:, None]
    )
    query_heads = queries.reshape(token_count, dec_heads, DHD)
    key_heads = keys.reshape(window_rows, dec_heads, DHD)
    value_heads = values.reshape(window_rows, dec_heads, DHD)
    scores = jnp.einsum(
        "thd,khd->htk", query_heads, key_heads, preferred_element_type=jnp.float32
    ) * DHD ** (-0.5)
    scores = jnp.where(allowed[None], scores, -jnp.inf)
    row_max = jnp.max(scores, axis=-1, keepdims=True)
    exponent = jnp.exp(scores - row_max)
    probs = (exponent / jnp.sum(exponent, axis=-1, keepdims=True)).astype(jnp.bfloat16)
    mixed = jnp.einsum("htk,khd->thd", probs, value_heads, preferred_element_type=jnp.float32)
    attended = mixed.astype(jnp.bfloat16).reshape(token_count, query_width)
    return (encoded, attended)


def solution(mesh):
    placed = (
        P(("dp", "frames"), "tok"),
        P(("dp", "frames"), None),
        P(("dp", "frames"), None),
        P(None, "tok", ("dp", "frames")),
        P("tok"),
        P(None, "tok"),
        P(None, "tok"),
        P(("dp", "frames"), "tok"),
        P(("dp", "frames")),
        P(("dp", "frames")),
    )
    return jax.shard_map(
        local,
        mesh=mesh,
        in_specs=placed,
        out_specs=(P(("dp", "frames"), "tok"), P(("dp", "frames"), "tok")),
        check_vma=False,
    )
```

profile of v0, /device:TPU:382, one launch (start us, length us, event | category | flops | bytes accessed | tf_op | source)
XLA Modules:
  0.0 492.5 jit_solution(14952448554756107410)
XLA Ops:
  12.2 1.6 fusion.28
  13.8 1.3 dynamic-slice.9
  16.3 132.1 %all-reduce.2 = (f32[512]{0:T(512)S(1)}, f32[512]{0:T(512)S(1)}) all-reduce(f32[512]{0:T(512)S(1)} %dynamic-update-slice.5, f32[512]{0:T(512)S(1)} %dynamic-update-slice.4), channel_id=4, replica_groups=mesh['frames'=64,'tok'=2,'dp'=4] {'frames'}, use_global_device_ids=true, to_apply=%add.1 | all-reduce | flops 1024 | bytes 8192
  152.0 5.0 %select_add_fusion = (s32[256]{0:T(256)S(1)}, s32[256]{0:T(256)S(1)}) fusion(s32[]{:T(128)} %bitcast.32, s32[]{:T(128)} %bitcast.31, s32[]{:T(128)} %bitcast.30, s32[]{:T(128)} %bitcast.29, s32[2,128]{1,0:T(2,128)S(1)} %copy-done.5, s32[2]{0:T(128)S(1)} %iota_multiply_fusion, s32[]{:T(128)} %bitcast.28, s32[]{:T(128)} %bitcast.27, s32[]{:T(128)} %bitcast.26, ...), kind=kLoop, calls=%fused_computation.69 | loop fusion | flops 5120 | bytes 3112 | tf_op jit(solution)/shard_map/add | solution.py:119
  157.0 44.6 %all-gather.9.cloned.1.call-done = f32[512,64,128]{2,1,0:T(8,128)} async-done(((f32[8,64,128]{2,1,0:T(8,128)}), f32[512,64,128]{2,1,0:T(8,128)}) %all-gather.9.cloned.1.call-update) | async-done | bytes 16777232 | tf_op jit(solution)/shard_map/all_gather | solution.py:13
  201.6 4.4 while.29
  206.8 187.8 %all-gather.7.cloned.1.call-done = f32[512,64,128]{2,1,0:T(8,128)} async-done(((f32[8,64,128]{2,1,0:T(8,128)}), f32[512,64,128]{2,1,0:T(8,128)}) %all-gather.7.cloned.1.call-update) | async-done | bytes 16777232 | tf_op jit(solution)/shard_map/all_gather | solution.py:13
  394.6 65.3 %while.28 = (s32[]{:T(128)}, f32[8,64,128]{2,1,0:T(8,128)S(1)}, s32[]{:T(128)}, f32[64,8]{1,0:T(8,128)S(1)}, f32[64,8,64,128]{3,2,1,0:T(8,128)}, /*index=5*/s32[]{:T(128)}, s32[]{:T(128)}, s32[]{:T(128)}) while((s32[]{:T(128)}, f32[8,64,128]{2,1,0:T(8,128)S(1)}, s32[]{:T(128)}, f32[64,8]{1,0:T(8,128)S(1)}, f32[64,8,64,128]{3,2,1,0:T(8,128)}, ...), condition=%wide.region_2.3_spmd, body=%wide.region_1.2_spmd.sunk | while | flops 131077 | bytes 786655 | solution.py:22
  394.7 1.1 bitcast_add_fusion.4
  396.9 1.1 bitcast_add_fusion.4
  399.1 1.1 bitcast_add_fusion.4
  401.3 1.1 bitcast_add_fusion.4
  402.4 1.1 bitcast_add_fusion.4
  404.6 1.1 bitcast_add_fusion.4
  406.8 1.1 bitcast_add_fusion.4
  407.9 1.1 bitcast_add_fusion.4
  409.0 1.1 bitcast_add_fusion.4
  460.6 2.0 all_gather.29
  462.7 4.9 collective-permute-start
  467.6 1.9 collective-permute-start.1
  470.4 3.0 collective-permute-done
  473.4 5.3 %collective-permute-done.1 = bf16[64,1024]{0,1:T(8,128)(2,1)S(1)} collective-permute-done((bf16[64,1024]{0,1:T(8,128)(2,1)S(1)}, bf16[64,1024]{0,1:T(8,128)(2,1)S(1)}, u32[]{:S(2)}, u32[]{:S(2)}) %collective-permute-start.1) | collective-permute-done | bytes 131104 | tf_op jit(solution)/shard_map/ppermute | solution.py:35
  479.9 2.3 convolution_convert_fusion.1
  483.4 1.3 fusion.6
  (177 shorter events, 72.4 us)
Async XLA Ops:
  7.2 471.6 %copy-start = (bf16[1024,640]{1,0:T(8,128)(2,1)S(1)}, bf16[1024,640]{1,0:T(8,128)(2,1)}, u32[]{:S(2)}) copy-start(bf16[1024,640]{1,0:T(8,128)(2,1)} %param.25) | copy-start | bytes 3932164
  7.2 144.8 %copy-start.5 = (s32[2,128]{1,0:T(2,128)S(1)}, s32[2,128]{1,0:T(2,128)}, u32[]{:S(2)}) copy-start(s32[2,128]{1,0:T(2,128)} %constant.156.clone.1) | copy-start | bytes 3076
  7.2 143.2 %copy-start.1 = (bf16[256,640]{1,0:T(8,128)(2,1)S(1)}, bf16[256,640]{1,0:T(8,128)(2,1)}, u32[]{:S(2)}) copy-start(bf16[256,640]{1,0:T(8,128)(2,1)} %param.27) | copy-start | bytes 983044
  7.2 143.4 %copy-start.3 = (s32[4]{0:T(128)S(1)}, s32[4]{0:T(128)}, u32[]{:S(2)}) copy-start(s32[4]{0:T(128)} %param.28) | copy-start | bytes 52
  7.2 144.1 %copy-start.4 = (s32[4]{0:T(128)S(1)}, s32[4]{0:T(128)}, u32[]{:S(2)}) copy-start(s32[4]{0:T(128)} %param.29) | copy-start | bytes 52
  7.2 194.4 %all-gather.9.cloned.1.call-start = ((), (), s32[]{:S(2)}) async-start(), calls=%async_computation.1 | async-start | bytes 17039360 | tf_op jit(solution)/shard_map/all_gather | solution.py:13
  11.6 383.0 %all-gather.7.cloned.1.call-start = ((), (), s32[]{:S(2)}) async-start(), calls=%async_computation | async-start | bytes 17039360 | tf_op jit(solution)/shard_map/all_gather | solution.py:13
  206.6 253.3 %copy-start.2 = (bf16[128,128]{1,0:T(8,128)(2,1)S(1)}, bf16[128,128]{1,0:T(8,128)(2,1)}, u32[]{:S(2)}) copy-start(bf16[128,128]{1,0:T(8,128)(2,1)} %param.22) | copy-start | bytes 98308
  206.7 253.5 %copy-start.6 = (f32[8]{0:T(128)S(1)}, f32[8]{0:T(128)}, u32[]{:S(2)}) copy-start(f32[8]{0:T(128)} %param.24) | copy-start | bytes 100
  462.7 10.7 %collective-permute-start = (bf16[64,1024]{0,1:T(8,128)(2,1)S(1)}, bf16[64,1024]{0,1:T(8,128)(2,1)S(1)}, u32[]{:S(2)}, u32[]{:S(2)}) collective-permute-start(bf16[64,1024]{0,1:T(8,128)(2,1)S(1)} %get-tuple-element.187), channel_id=1, source_target_pairs={{0,8},{8,16},{16,24},{24,32},{32,40},{40,48},{48,56},{56,64},{64,7... | collective-permute-start | bytes 393224 | tf_op jit(solution)/shard_map/ppermute | solution.py:33
  467.6 11.2 %collective-permute-start.1 = (bf16[64,1024]{0,1:T(8,128)(2,1)S(1)}, bf16[64,1024]{0,1:T(8,128)(2,1)S(1)}, u32[]{:S(2)}, u32[]{:S(2)}) collective-permute-start(bf16[64,1024]{0,1:T(8,128)(2,1)S(1)} %get-tuple-element.188), channel_id=1, source_target_pairs={{8,0},{16,8},{24,16},{32,24},{40,32},{48,40},{56,48},{64,56},{72,6... | collective-permute-start | bytes 393224 | tf_op jit(solution)/shard_map/ppermute | solution.py:35
Sparse Core Ops, SparseCore 0:
  11.7 189.8 all-gather.8
  204.5 189.9 all-gather.6
where the time goes:
time: 495 us; the launch traced here: 492 us
  waiting for transfers between devices  241 us (49%)
  blocking collectives  134 us (27%)
  other arithmetic  72.7 us (15%)
  between operations  15 us (3%)
  local copies, waits for them, and re-layouts  10.6 us (2%)
  matrix products  10.1 us (2%)
  starting transfers between devices  6.88 us (1%)
    all_gather x2, waiting for transfers between devices, entering(): gathered = jax.tree.map(lambda a: lax.all_gather(a, axis), part)  232 us
    unnamed x1, blocking collectives  132 us
    add x63, other arithmetic, chain_combine(): later[0][:, None, None] * earlier[1] + later[1]  66.8 us
  transfers between devices with their start and end apart: 4, of which 4 were waited for; matrix products, arithmetic and copies ran while one was open for 4% of the time, Pallas kernels for 0%

commit v1 on v0

v1 whole, which is shorter than its diff:
```python
import functools

import jax
import jax.numpy as jnp
from jax import lax
from jax.experimental import pallas as pl
from jax.experimental.pallas import tpu as pltpu
from jax.sharding import PartitionSpec as P

DHD = 64
F = 128
RIM = 64
N = 128
HD = 64
NI = 4
HP = 2
PIECE = HP * HD
MESH = pl.DeviceIdType.MESH
HIGH = lax.Precision.HIGHEST
NT = (((1,), (1,)), ((), ()))
BF = jnp.bfloat16
F32 = jnp.float32


def dot(a, b):
    return jnp.dot(a, b, preferred_element_type=F32)


def dot_nt(a, b, precision=None):
    return lax.dot_general(a, b, NT, precision=precision, preferred_element_type=F32)


def tall(tile, first):
    return jnp.concatenate(
        [jnp.broadcast_to(tile[first + k : first + k + 1], (HD, N)) for k in range(HP)], axis=0
    )


def mixer(
    dims,
    x_hbm,
    b_hbm,
    c_hbm,
    ld_hbm,
    gain_hbm,
    wk_hbm,
    wv_hbm,
    q_hbm,
    start_hbm,
    len_hbm,
    wide,
    keys,
    values,
    q_out,
    bias,
    xv,
    bv,
    cv,
    ldv,
    gain,
    starts,
    lens,
    wk,
    wv,
    lsend,
    lrecv,
    crx,
    ldrx,
    gsend,
    grecv,
    gtsend,
    gtrecv,
    ysend,
    yrecv,
    ytsend,
    ytrecv,
    csend,
    crecv,
    pre,
    prebf,
    rim_l,
    rim_r,
    within,
    grown,
    local_part,
    rwin,
    rin,
    rx,
    kacc,
    vacc,
    hsem,
    ssem,
    rsem,
):
    ny, ng, tok_count = dims
    heads = ldv.shape[1]
    half = xv.shape[1]
    sub = PIECE // ng
    frames = ny * ng * NI
    row = ng * NI
    me = lax.axis_index("frames")
    tok = lax.axis_index("tok")
    y = me // row
    g = lax.rem(me // NI, ng)
    i = lax.rem(me, NI)
    base = me - i

    def at_i(p):
        return base + p

    def at_g(p):
        return me + (p - g) * NI

    def at_y(p):
        return me + (p - y) * row

    prev = lax.rem(me + frames - 1, frames)
    succ = lax.rem(me + 1, frames)
    base_prev = lax.rem(base + frames - NI, frames)
    base_succ = lax.rem(base + NI, frames)

    fetched = {}

    def fetch(name, src, dst):
        copy = pltpu.make_async_copy(src, dst, hsem.at[len(fetched)])
        copy.start()
        fetched[name] = copy

    fetch("ld", ld_hbm, ldv)
    fetch("x", x_hbm, xv)
    fetch("b", b_hbm, bv)
    fetch("c", c_hbm, cv)
    fetch("gain", gain_hbm, gain)
    fetch("start", start_hbm, starts)
    fetch("len", len_hbm, lens)
    fetch("wk", wk_hbm, wk)
    fetch("wv", wv_hbm, wv)
    fetch("q", q_hbm, q_out)

    barrier = pltpu.get_barrier_semaphore()

    def greet(**device):
        pl.semaphore_signal(barrier, inc=1, device_id=device, device_id_type=MESH)

    greeted = 0
    for own, count, place in ((i, NI, at_i), (g, ng, at_g), (y, ny, at_y)):
        for k in range(1, count):
            greet(frames=place(lax.rem(own + k, count)))
            greeted += 1
    greet(frames=prev)
    greet(frames=succ)
    greeted += 2
    if tok_count > 1:
        greet(tok=1 - tok)
        greeted += 1

    @pl.when(i == 0)
    def _():
        for k in range(NI):
            greet(frames=base_prev + k)

    @pl.when(i == NI - 1)
    def _():
        for k in range(NI):
            greet(frames=base_succ + k)

    greeted += 2

    sent = []
    taken = [0]

    def take(n):
        first = taken[0]
        taken[0] += n
        return first

    def remote(src, dst, index, device, landing=None):
        return pltpu.make_async_remote_copy(
            src_ref=src,
            dst_ref=dst,
            send_sem=ssem.at[index],
            recv_sem=rsem.at[index if landing is None else landing],
            device_id=device,
            device_id_type=MESH,
        )

    def start(copy):
        copy.start()
        sent.append(copy)

    def scatter(own, count, place, src, dst, first):
        for k in range(1, count):
            p = lax.rem(own + k, count)
            start(remote(src.at[p], dst.at[own], first + k - 1, {"frames": place(p)}))

    def share(own, count, place, src, dst, first):
        for k in range(1, count):
            p = lax.rem(own + k, count)
            start(remote(src, dst.at[own], first + k - 1, {"frames": place(p)}))

    def arrive(own, count, place, src, dst, first):
        for k in range(1, count):
            q = lax.rem(own + count - k, count)
            remote(src, dst.at[q], first + k - 1, {"frames": place(q)}).wait_recv()

    sem_ld, sem_c = take(NI - 1), take(NI - 1)
    sem_l = (take(NI - 1), take(NI - 1))
    sem_gt = take(ng - 1)
    sem_g = (take(ng - 1), take(ng - 1))
    sem_yt = take(ny - 1)
    sem_y = (take(ny - 1), take(ny - 1))
    sem_b = (take(ng - 1), take(ng - 1))
    sem_rim = take(2)
    sem_r = take(NI - 1)
    sem_rx = take(NI)
    sem_w = take(NI)

    pl.semaphore_wait(barrier, greeted)
    share(i, NI, at_i, ld_hbm, ldrx, sem_ld)
    share(i, NI, at_i, c_hbm, crx, sem_c)

    r_id = lax.broadcasted_iota(jnp.int32, (F, F), 0)
    s_id = lax.broadcasted_iota(jnp.int32, (F, F), 1)
    fetched["ld"].wait()
    ld_f = ldv[0]
    ld_b = ldv[1]
    tail_f = jnp.dot(ld_f, (r_id > s_id).astype(F32), precision=HIGH, preferred_element_type=F32)
    row_b = jnp.dot(ld_b, (r_id < s_id).astype(F32), precision=HIGH, preferred_element_type=F32)
    to_end = (jnp.exp(tail_f), jnp.exp(row_b))
    fetched["x"].wait()
    fetched["b"].wait()
    turned = []
    for d in range(2):
        for p in range(NI):
            if d == 0:
                turned.append(xv[:, p * PIECE : (p + 1) * PIECE].astype(F32).T)
            scaled = (turned[p] * tall(to_end[d], p * HP)).astype(BF)
            lsend[d, p] = dot(scaled, bv[...]).astype(BF)
        scatter(i, NI, at_i, lsend.at[d], lrecv.at[d], sem_l[d])
        lrecv[d, pl.ds(i, 1)] = lsend[d, pl.ds(i, 1)]

    fetched["c"].wait()
    fetched["gain"].wait()
    crx[pl.ds(i, 1)] = cv[...][None]
    ldrx[pl.ds(i, 1)] = ldv[...][None]
    gram = dot_nt(cv[...], bv[...])
    gram = jnp.where(r_id == s_id, 2.0 * gram, gram)
    row_f = jnp.dot(ld_f, (r_id <= s_id).astype(F32), precision=HIGH, preferred_element_type=F32)
    lower = s_id <= r_id
    col_f = dot_nt(lower.astype(F32), ld_f, HIGH)
    col_b = dot_nt((s_id < r_id).astype(F32), ld_b, HIGH)
    left = s_id < HD
    for p in range(NI):
        x_pair = xv[:, p * PIECE : (p + 1) * PIECE].astype(F32)
        weights = []
        for h in range(HP * p, HP * p + HP):
            at_f = jnp.broadcast_to(col_f[:, h : h + 1], (F, F))
            at_b = jnp.broadcast_to(col_b[:, h : h + 1], (F, F))
            exponent = jnp.where(lower, at_f - row_f[h : h + 1], row_b[h : h + 1] - at_b)
            weights.append((jnp.exp(exponent) * gram).astype(BF))
        apart = jnp.concatenate(
            [jnp.where(left, x_pair, 0.0), jnp.where(left, 0.0, x_pair)], axis=0
        ).astype(BF)
        intra = dot(jnp.concatenate(weights, axis=1), apart)
        inside = intra + jnp.where(left[0:1], gain[HP * p], gain[HP * p + 1]) * x_pair
        pre[p] = inside
        prebf[p] = inside.astype(BF)
    rims = (
        remote(prebf.at[:, 0:RIM], rim_r, sem_rim, {"frames": prev}),
        remote(prebf.at[:, RIM:F], rim_l, sem_rim + 1, {"frames": succ}),
    )
    for copy in rims:
        start(copy)

    rows, tots, decays = [], [], []
    state_of = [None, None]

    def group_states(d):
        if d == 0:
            arrive(i, NI, at_i, ld_hbm, ldrx, sem_ld)
            for j in range(NI):
                picked = jnp.concatenate(
                    [
                        functools.reduce(
                            lambda a, p: jnp.where(i == p, ldrx[j, e, HP * p : HP * p + HP, :], a),
                            range(1, NI),
                            ldrx[j, e, 0:HP, :],
                        )
                        for e in range(2)
                    ],
                    axis=0,
                )
                rows.append(picked)
                tots.append(
                    jnp.broadcast_to(jnp.sum(picked, axis=1, keepdims=True), (2 * HP, N))
                )
                decays.append(jnp.exp(tots[j]))
            gtsend[...] = jnp.concatenate(
                [functools.reduce(jnp.add, tots), jnp.zeros((8 - 2 * HP, N), F32)], axis=0
            )
            share(g, ng, at_g, gtsend, gtrecv, sem_gt)
            gtrecv[g] = gtsend[...]
        arrive(i, NI, at_i, lsend.at[d, 0], lrecv.at[d], sem_l[d])
        state = jnp.zeros((PIECE, N), F32)
        for j in range(NI) if d == 0 else reversed(range(NI)):
            within[d, j] = state.astype(BF)
            state = tall(decays[j], d * HP) * state + lrecv[d, j].astype(F32)
        for k in range(ng):
            gsend[d, k] = state[k * sub : (k + 1) * sub].astype(BF)
        scatter(g, ng, at_g, gsend.at[d], grecv.at[d], sem_g[d])
        grecv[d, pl.ds(g, 1)] = gsend[d, pl.ds(g, 1)]

    group_tots = [[], []]
    into = [[None] * ng, [None] * ng]
    ahead = [[None] * ng, [None] * ng]

    def row_states(d):
        if d == 0:
            arrive(g, ng, at_g, gtsend, gtrecv, sem_gt)
            head = (g * sub) // HD
            for k in range(ng):
                for e in range(2):
                    one = gtrecv[k, e * HP : e * HP + 1, :]
                    for h in range(1, HP):
                        one = jnp.where(head == h, gtrecv[k, e * HP + h : e * HP + h + 1, :], one)
                    group_tots[e].append(one)
            if ny > 1:
                ytsend[...] = jnp.concatenate(
                    [functools.reduce(jnp.add, group_tots[e]) for e in range(2)]
                    + [jnp.zeros((6, N), F32)],
                    axis=0,
                )
                share(y, ny, at_y, ytsend, ytrecv, sem_yt)
                ytrecv[y] = ytsend[...]
        arrive(g, ng, at_g, gsend.at[d, 0], grecv.at[d], sem_g[d])
        state, total = jnp.zeros((sub, N), F32), jnp.zeros((1, N), F32)
        for k in range(ng) if d == 0 else reversed(range(ng)):
            into[d][k], ahead[d][k] = state, jnp.exp(total)
            state = jnp.exp(group_tots[d][k]) * state + grecv[d, k].astype(F32)
            total = total + group_tots[d][k]
        if ny > 1:
            ysend[d] = state.astype(BF)
            share(y, ny, at_y, ysend.at[d], yrecv.at[d], sem_y[d])
            yrecv[d, pl.ds(y, 1)] = ysend[d][None]

    def entering(d):
        enter = jnp.zeros((sub, N), F32)
        if ny > 1:
            if d == 0:
                arrive(y, ny, at_y, ytsend, ytrecv, sem_yt)
            arrive(y, ny, at_y, ysend.at[d], yrecv.at[d], sem_y[d])
            state = jnp.zeros((sub, N), F32)
            for k in range(ny) if d == 0 else reversed(range(ny)):
                enter = jnp.where(y == k, state, enter)
                state = jnp.exp(ytrecv[k, d : d + 1, :]) * state + yrecv[d, k].astype(F32)
        for k in range(ng):
            csend[d, k] = (into[d][k] + ahead[d][k] * enter).astype(BF)
        scatter(g, ng, at_g, csend.at[d], crecv.at[d], sem_b[d])
        crecv[d, pl.ds(g, 1)] = csend[d, pl.ds(g, 1)]

    group_states(0)
    group_states(1)

    arrive(i, NI, at_i, c_hbm, crx, sem_c)
    picked_f = jnp.concatenate([r[0:HP] for r in rows], axis=0)
    picked_b = jnp.concatenate([r[HP : 2 * HP] for r in rows], axis=0)
    cols = (
        dot_nt(lower.astype(F32), picked_f, HIGH),
        dot_nt((s_id >= r_id).astype(F32), picked_b, HIGH),
    )

    def group_terms(d):
        total = jnp.zeros((2 * HP, N), F32)
        for j in range(NI) if d == 0 else reversed(range(NI)):
            at = [jnp.broadcast_to(cols[d][:, HP * j + h : HP * j + h + 1], (F, F)) for h in range(HP)]
            spread = jnp.exp(jnp.where(left, at[0], at[1]))
            lead = jnp.exp(
                jnp.where(left[0:1], total[d * HP : d * HP + 1], total[d * HP + 1 : d * HP + 2])
            )
            grown[d, j] = spread * lead
            part = spread * dot_nt(crx[j], within[d, j])
            local_part[j] = part if d == 0 else local_part[j] + part
            total = total + tots[j]

    group_terms(0)
    row_states(0)
    row_states(1)
    group_terms(1)
    entering(0)
    entering(1)

    fetched["start"].wait()
    fetched["len"].wait()
    groups = starts.shape[0]
    tokens, window = bias.shape
    per_group = tokens // groups
    place = lax.broadcasted_iota(jnp.int32, (per_group, window), 1) + (me * F - RIM)
    for k in range(groups):
        allowed = (place >= starts[k]) & (place < starts[k] + lens[k])
        bias[k * per_group : (k + 1) * per_group, :] = jnp.where(allowed, 0.0, -jnp.inf)
    rwin[0:RIM] = jnp.zeros((RIM, N), BF)
    rwin[RIM + NI * F :] = jnp.zeros((RIM, N), BF)

    for d in range(2):
        arrive(g, ng, at_g, csend.at[d, 0], crecv.at[d], sem_b[d])
        carried = crecv[d].reshape(PIECE, N)
        for j in range(NI):
            part = local_part[j] + grown[d, j] * dot_nt(crx[j], carried)
            if d == 0:
                local_part[j] = part
            else:
                rwin[RIM + j * F : RIM + (j + 1) * F] = part.astype(BF)
    for k in range(1, NI):
        p = lax.rem(i + k, NI)
        src = rwin.at[pl.ds(pl.multiple_of(p * F, F), 2 * F)]
        start(remote(src, rin.at[i], sem_r + k - 1, {"frames": at_i(p)}))
    start(
        remote(rwin.at[RIM : 2 * RIM], rx.at[i], sem_rx, {"frames": base_prev + NI - 1}, sem_rx + i)
    )
    start(
        remote(rwin.at[NI * F : NI * F + RIM], rx.at[i], sem_rx + 1, {"frames": base_succ}, sem_rx + i)
    )
    rin[pl.ds(i, 1)] = rwin[pl.ds(pl.multiple_of(i * F, F), 2 * F)][None]
    remote(prebf.at[:, 0:RIM], rim_r, sem_rim, {"frames": prev}).wait_recv()
    remote(prebf.at[:, RIM:F], rim_l, sem_rim + 1, {"frames": succ}).wait_recv()

    def rows_in(q):
        remote(rwin.at[0:RIM], rx.at[q], sem_rx, {"frames": prev}, sem_rx + q).wait_recv()

    for k in range(NI):
        q = lax.rem(i + NI - k, NI)
        if k > 0:
            remote(
                rwin.at[0 : 2 * F], rin.at[q], sem_r + k - 1, {"frames": at_i(q)}
            ).wait_recv()

        @pl.when((i == 0) | (i == NI - 1))
        def _():
            rows_in(q)

        @pl.when(i == 0)
        def _():
            rin[q, 0:RIM] = rx[q]

        @pl.when(i == NI - 1)
        def _():
            rin[q, RIM + F :] = rx[q]

        wide[tok, q, 0:RIM] = (rim_l[q].astype(F32) + rin[q, 0:RIM].astype(F32)).astype(BF)
        wide[tok, q, RIM : RIM + F] = (pre[q] + rin[q, RIM : RIM + F].astype(F32)).astype(BF)
        wide[tok, q, RIM + F :] = (rim_r[q].astype(F32) + rin[q, RIM + F :].astype(F32)).astype(BF)
        if tok_count > 1:
            start(remote(wide.at[tok, q], wide.at[tok, q], sem_w + k, {"tok": 1 - tok}))

    fetched["wk"].wait()
    fetched["wv"].wait()

    def half_rows(t):
        return jnp.concatenate([wide[t, p] for p in range(NI)], axis=1)

    mine = half_rows(tok)
    at = pl.ds(pl.multiple_of(tok * half, half), half)
    kacc[...] = dot(mine, wk[at, :])
    vacc[...] = dot(mine, wv[at, :])
    if tok_count > 1:
        other = 1 - tok
        for k in range(NI):
            q = lax.rem(i + NI - k, NI)
            remote(wide.at[tok, q], wide.at[other, q], sem_w + k, {"tok": other}).wait_recv()
        theirs = half_rows(other)
        at = pl.ds(pl.multiple_of(other * half, half), half)
        keys[...] = (kacc[...] + dot(theirs, wk[at, :])).astype(BF)
        values[...] = (vacc[...] + dot(theirs, wv[at, :])).astype(BF)
    else:
        keys[...] = kacc[...].astype(BF)
        values[...] = vacc[...].astype(BF)
    fetched["q"].wait()
    for copy in sent:
        copy.wait_send()


def reader(wide, keys, values, queries, bias, enc_ref, out_ref):
    tok = lax.axis_index("tok")
    for p in range(NI):
        enc_ref[:, p * PIECE : (p + 1) * PIECE] = wide[tok, p, RIM : RIM + F]
    left = lax.broadcasted_iota(jnp.int32, (1, 2 * DHD), 1) < DHD
    for p in range(queries.shape[1] // (2 * DHD)):
        cols = slice(p * 2 * DHD, (p + 1) * 2 * DHD)
        q_pair = queries[:, cols]
        k_pair = keys[:, cols].astype(F32)
        v_pair = values[:, cols]
        both = []
        for only in (jnp.where(left, k_pair, 0.0), jnp.where(left, 0.0, k_pair)):
            scores = dot_nt(q_pair, only.astype(BF)) + bias[...]
            top = jnp.max(scores, axis=1, keepdims=True)
            raised = jnp.exp((scores - top) * DHD ** (-0.5))
            whole = 1.0 / jnp.sum(raised, axis=1, keepdims=True)
            both.append(dot((raised * whole).astype(BF), v_pair))
        out_ref[:, cols] = jnp.where(left, both[0], both[1]).astype(BF)


def solution(mesh):
    frames = mesh.shape["frames"]
    tok_count = mesh.shape["tok"]
    ng = min(4, frames // NI)
    ny = frames // (NI * ng)
    sub = PIECE // ng
    vmem = pl.BlockSpec(memory_space=pltpu.VMEM)
    hbm = pl.BlockSpec(memory_space=pltpu.HBM)

    def local(x, b, c, log_decay, gain, key_weight, value_weight, queries, span_start, span_len):
        count, width = x.shape
        window = 2 * count
        tokens, out_width = queries.shape
        copies = 5 * (NI - 1) + 5 * (ng - 1) + 3 * (ny - 1) + 2 + 2 * NI
        wide, keys, values, held, bias = pl.pallas_call(
            functools.partial(mixer, (ny, ng, tok_count)),
            out_shape=(
                jax.ShapeDtypeStruct((tok_count, NI, window, PIECE), BF),
                jax.ShapeDtypeStruct((window, out_width), BF),
                jax.ShapeDtypeStruct((window, out_width), BF),
                jax.ShapeDtypeStruct(queries.shape, BF),
                jax.ShapeDtypeStruct((tokens, window), F32),
            ),
            in_specs=[hbm] * 10,
            out_specs=(vmem,) * 5,
            scratch_shapes=[
                pltpu.VMEM(x.shape, BF),
                pltpu.VMEM(b.shape, BF),
                pltpu.VMEM(c.shape, BF),
                pltpu.VMEM(log_decay.shape, F32),
                pltpu.SMEM(gain.shape, F32),
                pltpu.SMEM(span_start.shape, jnp.int32),
                pltpu.SMEM(span_len.shape, jnp.int32),
                pltpu.VMEM(key_weight.shape, BF),
                pltpu.VMEM(value_weight.shape, BF),
                pltpu.VMEM((2, NI, PIECE, N), BF),
                pltpu.VMEM((2, NI, PIECE, N), BF),
                pltpu.VMEM((NI,) + c.shape, BF),
                pltpu.VMEM((NI,) + log_decay.shape, F32),
                pltpu.VMEM((2, ng, sub, N), BF),
                pltpu.VMEM((2, ng, sub, N), BF),
                pltpu.VMEM((8, N), F32),
                pltpu.VMEM((ng, 8, N), F32),
                pltpu.VMEM((2, sub, N), BF),
                pltpu.VMEM((2, ny, sub, N), BF),
                pltpu.VMEM((8, N), F32),
                pltpu.VMEM((ny, 8, N), F32),
                pltpu.VMEM((2, ng, sub, N), BF),
                pltpu.VMEM((2, ng, sub, N), BF),
                pltpu.VMEM((NI, count, PIECE), F32),
                pltpu.VMEM((NI, count, PIECE), BF),
                pltpu.VMEM((NI, RIM, PIECE), BF),
                pltpu.VMEM((NI, RIM, PIECE), BF),
                pltpu.VMEM((2, NI, PIECE, N), BF),
                pltpu.VMEM((2, NI, count, PIECE), F32),
                pltpu.VMEM((NI, count, PIECE), F32),
                pltpu.VMEM((2 * RIM + NI * count, PIECE), BF),
                pltpu.VMEM((NI, window, PIECE), BF),
                pltpu.VMEM((NI, RIM, PIECE), BF),
                pltpu.VMEM((window, out_width), F32),
                pltpu.VMEM((window, out_width), F32),
                pltpu.SemaphoreType.DMA((10,)),
                pltpu.SemaphoreType.DMA((copies,)),
                pltpu.SemaphoreType.DMA((copies,)),
            ],
            compiler_params=pltpu.CompilerParams(
                collective_id=0, has_side_effects=True, vmem_limit_bytes=24 * 2**20
            ),
        )(
            *(
                pltpu.with_memory_space_constraint(a, pltpu.HBM)
                for a in (
                    x,
                    b,
                    c,
                    log_decay,
                    gain,
                    key_weight,
                    value_weight,
                    queries,
                    span_start,
                    span_len,
                )
            )
        )
        return pl.pallas_call(
            reader,
            out_shape=(
                jax.ShapeDtypeStruct((count, width), BF),
                jax.ShapeDtypeStruct(queries.shape, BF),
            ),
            in_specs=[vmem] * 5,
            out_specs=(vmem, vmem),
            compiler_params=pltpu.CompilerParams(vmem_limit_bytes=24 * 2**20),
        )(wide, keys, values, held, bias)

    placed = (
        P(("dp", "frames"), "tok"),
        P(("dp", "frames"), None),
        P(("dp", "frames"), None),
        P(None, "tok", ("dp", "frames")),
        P("tok"),
        P(None, "tok"),
        P(None, "tok"),
        P(("dp", "frames"), "tok"),
        P(("dp", "frames")),
        P(("dp", "frames")),
    )
    return jax.shard_map(
        local,
        mesh=mesh,
        in_specs=placed,
        out_specs=(P(("dp", "frames"), "tok"), P(("dp", "frames"), "tok")),
        check_vma=False,
    )
```

time: 495 us -> 60.1 us (0.12)
  the two profiles are of different devices: /device:TPU:382 before, /device:TPU:1 now
where the time goes in v1:
time: 60.1 us; the launch traced here: 60 us
  Pallas kernels  59.3 us (99%)
  between operations  0.64 us (1%)
    pallas_call x1, Pallas kernels, local(): pl.pallas_call(functools.partial(mixer, (ny, ng, tok_count)), out_shape=(...  56.8 us
    pallas_call x1, Pallas kernels, local(): pl.pallas_call(reader, out_shape=(jax.ShapeDtypeStruct((count, width), BF...  2.56 us

profile of v1, /device:TPU:1, one launch (start us, length us, event | category | flops | bytes accessed | tf_op | source)
XLA Modules:
  0.0 60.0 jit_solution(11256081262667689713)
XLA Ops:
  0.6 56.8 %shard_map.113 = (bf16[2,4,256,128]{3,2,1,0:T(8,128)(2,1)S(1)}, bf16[256,640]{1,0:T(8,128)(2,1)S(1)}, bf16[256,640]{1,0:T(8,128)(2,1)S(1)}, bf16[256,640]{1,0:T(8,128)(2,1)S(1)}, f32[256,256]{1,0:T(8,128)S(1)}) custom-call(bf16[128,512]{1,0:T(8,128)(2,1)} %x_hbm.1, bf16[128,128]{1,0:T(8,128)(2,1)} %b_hbm.1, bf16[128,128]{1,0:T(8,128)(2,1)} %c_hbm.1, ...), custom_call_target="tpu_custom_call" | custom-call | tf_op jit(solution)/shard_map/pallas_call | solution.py:516
  57.4 2.6 %shard_map.114 = (bf16[128,512]{1,0:T(8,128)(2,1)}, bf16[256,640]{1,0:T(8,128)(2,1)}) custom-call(bf16[2,4,256,128]{3,2,1,0:T(8,128)(2,1)S(1)} %get-tuple-element.7.wide, bf16[256,640]{1,0:T(8,128)(2,1)S(1)} %get-tuple-element.8.keys, bf16[256,640]{1,0:T(8,128)(2,1)S(1)} %get-tuple-element.9.values, bf16[256,640]{1,0:T(8,128)(2,1)S(1)} %get-tuple-element.10.queries, ...), custom_call_target="tpu_custom_call" | custom-call | tf_op jit(solution)/shard_map/pallas_call | solution.py:587

commit v2 on v1

--- a/solution.py
+++ b/solution.py
@@ -12,8 +12,10 @@
 RIM = 64
 N = 128
 HD = 64
-NI = 4
-HP = 2
+NI = 2
+PAIRS = 4
+HP = 2 * PAIRS // NI
+LP = PAIRS // NI
 PIECE = HP * HD
 MESH = pl.DeviceIdType.MESH
 HIGH = lax.Precision.HIGHEST
@@ -28,6 +30,23 @@
 
 def dot_nt(a, b, precision=None):
     return lax.dot_general(a, b, NT, precision=precision, preferred_element_type=F32)
+
+
+def thirds(a):
+    high = a.astype(BF)
+    rest = a - high.astype(F32)
+    mid = rest.astype(BF)
+    return high, mid, (rest - mid.astype(F32)).astype(BF)
+
+
+def sum_rows(parts, mask):
+    both = dot(jnp.concatenate(parts, axis=0), mask.astype(BF))
+    n = parts[0].shape[0]
+    return both[0:n] + both[n : 2 * n] + both[2 * n : 3 * n]
+
+
+def sum_cols(mask, parts):
+    return functools.reduce(jnp.add, [dot_nt(mask.astype(BF), p) for p in reversed(parts)])
 
 
 def tall(tile, first):
@@ -222,21 +241,31 @@
     r_id = lax.broadcasted_iota(jnp.int32, (F, F), 0)
     s_id = lax.broadcasted_iota(jnp.int32, (F, F), 1)
     fetched["ld"].wait()
-    ld_f = ldv[0]
-    ld_b = ldv[1]
-    tail_f = jnp.dot(ld_f, (r_id > s_id).astype(F32), precision=HIGH, preferred_element_type=F32)
-    row_b = jnp.dot(ld_b, (r_id < s_id).astype(F32), precision=HIGH, preferred_element_type=F32)
-    to_end = (jnp.exp(tail_f), jnp.exp(row_b))
+    parts_f = thirds(ldv[0])
+    to_end = [jnp.exp(sum_rows(parts_f, (r_id > s_id).astype(F32))), None]
     fetched["x"].wait()
     fetched["b"].wait()
     turned = []
+    row_b = None
     for d in range(2):
+        if d == 1:
+            parts_b = thirds(ldv[1])
+            row_b = sum_rows(parts_b, (r_id < s_id).astype(F32))
+            to_end[1] = jnp.exp(row_b)
         for p in range(NI):
             if d == 0:
                 turned.append(xv[:, p * PIECE : (p + 1) * PIECE].astype(F32).T)
             scaled = (turned[p] * tall(to_end[d], p * HP)).astype(BF)
             lsend[d, p] = dot(scaled, bv[...]).astype(BF)
-        scatter(i, NI, at_i, lsend.at[d], lrecv.at[d], sem_l[d])
+
+            @pl.when(i != p)
+            def _():
+                slot = sem_l[d] + lax.rem(p - i + NI, NI) - 1
+                remote(lsend.at[d, p], lrecv.at[d, i], slot, {"frames": at_i(p)}).start()
+
+        for k in range(1, NI):
+            p = lax.rem(i + k, NI)
+            sent.append(remote(lsend.at[d, p], lrecv.at[d, i], sem_l[d] + k - 1, {"frames": at_i(p)}))
         lrecv[d, pl.ds(i, 1)] = lsend[d, pl.ds(i, 1)]
 
     fetched["c"].wait()
@@ -245,15 +274,15 @@
     ldrx[pl.ds(i, 1)] = ldv[...][None]
     gram = dot_nt(cv[...], bv[...])
     gram = jnp.where(r_id == s_id, 2.0 * gram, gram)
-    row_f = jnp.dot(ld_f, (r_id <= s_id).astype(F32), precision=HIGH, preferred_element_type=F32)
     lower = s_id <= r_id
-    col_f = dot_nt(lower.astype(F32), ld_f, HIGH)
-    col_b = dot_nt((s_id < r_id).astype(F32), ld_b, HIGH)
+    row_f = sum_rows(parts_f, (r_id <= s_id).astype(F32))
+    col_f = sum_cols(lower.astype(F32), parts_f)
+    col_b = sum_cols((s_id < r_id).astype(F32), parts_b)
     left = s_id < HD
-    for p in range(NI):
-        x_pair = xv[:, p * PIECE : (p + 1) * PIECE].astype(F32)
+    for p in range(PAIRS):
+        x_pair = xv[:, p * 2 * HD : (p + 1) * 2 * HD].astype(F32)
         weights = []
-        for h in range(HP * p, HP * p + HP):
+        for h in (2 * p, 2 * p + 1):
             at_f = jnp.broadcast_to(col_f[:, h : h + 1], (F, F))
             at_b = jnp.broadcast_to(col_b[:, h : h + 1], (F, F))
             exponent = jnp.where(lower, at_f - row_f[h : h + 1], row_b[h : h + 1] - at_b)
@@ -262,7 +291,7 @@
             [jnp.where(left, x_pair, 0.0), jnp.where(left, 0.0, x_pair)], axis=0
         ).astype(BF)
         intra = dot(jnp.concatenate(weights, axis=1), apart)
-        inside = intra + jnp.where(left[0:1], gain[HP * p], gain[HP * p + 1]) * x_pair
+        inside = intra + jnp.where(left[0:1], gain[2 * p], gain[2 * p + 1]) * x_pair
         pre[p] = inside
         prebf[p] = inside.astype(BF)
     rims = (
@@ -295,9 +324,9 @@
                     jnp.broadcast_to(jnp.sum(picked, axis=1, keepdims=True), (2 * HP, N))
                 )
                 decays.append(jnp.exp(tots[j]))
-            gtsend[...] = jnp.concatenate(
-                [functools.reduce(jnp.add, tots), jnp.zeros((8 - 2 * HP, N), F32)], axis=0
-            )
+            gtsend[0 : 2 * HP] = functools.reduce(jnp.add, tots)
+            if 2 * HP < 8:
+                gtsend[2 * HP :] = jnp.zeros((8 - 2 * HP, N), F32)
             share(g, ng, at_g, gtsend, gtrecv, sem_gt)
             gtrecv[g] = gtsend[...]
         arrive(i, NI, at_i, lsend.at[d, 0], lrecv.at[d], sem_l[d])
@@ -365,21 +394,24 @@
     picked_f = jnp.concatenate([r[0:HP] for r in rows], axis=0)
     picked_b = jnp.concatenate([r[HP : 2 * HP] for r in rows], axis=0)
     cols = (
-        dot_nt(lower.astype(F32), picked_f, HIGH),
-        dot_nt((s_id >= r_id).astype(F32), picked_b, HIGH),
+        sum_cols(lower.astype(F32), thirds(picked_f)),
+        sum_cols((s_id >= r_id).astype(F32), thirds(picked_b)),
     )
 
     def group_terms(d):
         total = jnp.zeros((2 * HP, N), F32)
         for j in range(NI) if d == 0 else reversed(range(NI)):
-            at = [jnp.broadcast_to(cols[d][:, HP * j + h : HP * j + h + 1], (F, F)) for h in range(HP)]
-            spread = jnp.exp(jnp.where(left, at[0], at[1]))
-            lead = jnp.exp(
-                jnp.where(left[0:1], total[d * HP : d * HP + 1], total[d * HP + 1 : d * HP + 2])
-            )
-            grown[d, j] = spread * lead
-            part = spread * dot_nt(crx[j], within[d, j])
-            local_part[j] = part if d == 0 else local_part[j] + part
+            for e in range(LP):
+                at = [
+                    jnp.broadcast_to(cols[d][:, HP * j + 2 * e + h : HP * j + 2 * e + h + 1], (F, F))
+                    for h in range(2)
+                ]
+                spread = jnp.exp(jnp.where(left, at[0], at[1]))
+                h = d * HP + 2 * e
+                lead = jnp.exp(jnp.where(left[0:1], total[h : h + 1], total[h + 1 : h + 2]))
+                grown[d, j, e] = spread * lead
+                part = spread * dot_nt(crx[j], within[d, j, e * N : (e + 1) * N])
+                local_part[j, e] = part if d == 0 else local_part[j, e] + part
             total = total + tots[j]
 
     group_terms(0)
@@ -398,40 +430,50 @@
     for k in range(groups):
         allowed = (place >= starts[k]) & (place < starts[k] + lens[k])
         bias[k * per_group : (k + 1) * per_group, :] = jnp.where(allowed, 0.0, -jnp.inf)
-    rwin[0:RIM] = jnp.zeros((RIM, N), BF)
-    rwin[RIM + NI * F :] = jnp.zeros((RIM, N), BF)
+    rwin[:, 0:RIM] = jnp.zeros((LP, RIM, N), BF)
+    rwin[:, RIM + NI * F :] = jnp.zeros((LP, RIM, N), BF)
 
     for d in range(2):
         arrive(g, ng, at_g, csend.at[d, 0], crecv.at[d], sem_b[d])
         carried = crecv[d].reshape(PIECE, N)
         for j in range(NI):
-            part = local_part[j] + grown[d, j] * dot_nt(crx[j], carried)
-            if d == 0:
-                local_part[j] = part
-            else:
-                rwin[RIM + j * F : RIM + (j + 1) * F] = part.astype(BF)
+            for e in range(LP):
+                part = local_part[j, e] + grown[d, j, e] * dot_nt(crx[j], carried[e * N : (e + 1) * N])
+                if d == 0:
+                    local_part[j, e] = part
+                else:
+                    rwin[e, RIM + j * F : RIM + (j + 1) * F] = part.astype(BF)
+
+    def pairs_of(q):
+        return pl.ds(q * LP, LP)
+
     for k in range(1, NI):
         p = lax.rem(i + k, NI)
-        src = rwin.at[pl.ds(pl.multiple_of(p * F, F), 2 * F)]
-        start(remote(src, rin.at[i], sem_r + k - 1, {"frames": at_i(p)}))
+        src = rwin.at[:, pl.ds(pl.multiple_of(p * F, F), 2 * F)]
+        start(remote(src, rin.at[pairs_of(i)], sem_r + k - 1, {"frames": at_i(p)}))
+    rim_there = rx.at[pairs_of(i)]
     start(
-        remote(rwin.at[RIM : 2 * RIM], rx.at[i], sem_rx, {"frames": base_prev + NI - 1}, sem_rx + i)
+        remote(rwin.at[:, RIM : 2 * RIM], rim_there, sem_rx, {"frames": base_prev + NI - 1}, sem_rx + i)
     )
     start(
-        remote(rwin.at[NI * F : NI * F + RIM], rx.at[i], sem_rx + 1, {"frames": base_succ}, sem_rx + i)
+        remote(
+            rwin.at[:, NI * F : NI * F + RIM], rim_there, sem_rx + 1, {"frames": base_succ}, sem_rx + i
+        )
     )
-    rin[pl.ds(i, 1)] = rwin[pl.ds(pl.multiple_of(i * F, F), 2 * F)][None]
+    rin[pairs_of(i)] = rwin[:, pl.ds(pl.multiple_of(i * F, F), 2 * F)]
     remote(prebf.at[:, 0:RIM], rim_r, sem_rim, {"frames": prev}).wait_recv()
     remote(prebf.at[:, RIM:F], rim_l, sem_rim + 1, {"frames": succ}).wait_recv()
 
     def rows_in(q):
-        remote(rwin.at[0:RIM], rx.at[q], sem_rx, {"frames": prev}, sem_rx + q).wait_recv()
+        remote(
+            rwin.at[:, 0:RIM], rx.at[pairs_of(q)], sem_rx, {"frames": prev}, sem_rx + q
+        ).wait_recv()
 
     for k in range(NI):
         q = lax.rem(i + NI - k, NI)
         if k > 0:
             remote(
-                rwin.at[0 : 2 * F], rin.at[q], sem_r + k - 1, {"frames": at_i(q)}
+                rwin.at[:, 0 : 2 * F], rin.at[pairs_of(q)], sem_r + k - 1, {"frames": at_i(q)}
             ).wait_recv()
 
         @pl.when((i == 0) | (i == NI - 1))
@@ -440,23 +482,26 @@
 
         @pl.when(i == 0)
         def _():
-            rin[q, 0:RIM] = rx[q]
+            rin[pairs_of(q), 0:RIM] = rx[pairs_of(q)]
 
         @pl.when(i == NI - 1)
         def _():
-            rin[q, RIM + F :] = rx[q]
-
-        wide[tok, q, 0:RIM] = (rim_l[q].astype(F32) + rin[q, 0:RIM].astype(F32)).astype(BF)
-        wide[tok, q, RIM : RIM + F] = (pre[q] + rin[q, RIM : RIM + F].astype(F32)).astype(BF)
-        wide[tok, q, RIM + F :] = (rim_r[q].astype(F32) + rin[q, RIM + F :].astype(F32)).astype(BF)
+            rin[pairs_of(q), RIM + F :] = rx[pairs_of(q)]
+
+        for e in range(LP):
+            m = q * LP + e
+            wide[tok, m, 0:RIM] = (rim_l[m].astype(F32) + rin[m, 0:RIM].astype(F32)).astype(BF)
+            wide[tok, m, RIM : RIM + F] = (pre[m] + rin[m, RIM : RIM + F].astype(F32)).astype(BF)
+            wide[tok, m, RIM + F :] = (rim_r[m].astype(F32) + rin[m, RIM + F :].astype(F32)).astype(BF)
         if tok_count > 1:
-            start(remote(wide.at[tok, q], wide.at[tok, q], sem_w + k, {"tok": 1 - tok}))
+            piece = wide.at[tok, pairs_of(q)]
+            start(remote(piece, piece, sem_w + k, {"tok": 1 - tok}))
 
     fetched["wk"].wait()
     fetched["wv"].wait()
 
     def half_rows(t):
-        return jnp.concatenate([wide[t, p] for p in range(NI)], axis=1)
+        return jnp.concatenate([wide[t, p] for p in range(PAIRS)], axis=1)
 
     mine = half_rows(tok)
     at = pl.ds(pl.multiple_of(tok * half, half), half)
@@ -466,7 +511,8 @@
         other = 1 - tok
         for k in range(NI):
             q = lax.rem(i + NI - k, NI)
-            remote(wide.at[tok, q], wide.at[other, q], sem_w + k, {"tok": other}).wait_recv()
+            piece = wide.at[other, pairs_of(q)]
+            remote(piece, piece, sem_w + k, {"tok": other}).wait_recv()
         theirs = half_rows(other)
         at = pl.ds(pl.multiple_of(other * half, half), half)
         keys[...] = (kacc[...] + dot(theirs, wk[at, :])).astype(BF)
@@ -479,10 +525,12 @@
         copy.wait_send()
 
 
-def reader(wide, keys, values, queries, bias, enc_ref, out_ref):
+def reader(wide, keys, values, queries, bias, enc_hbm, out_hbm, enc, out, sem):
     tok = lax.axis_index("tok")
-    for p in range(NI):
-        enc_ref[:, p * PIECE : (p + 1) * PIECE] = wide[tok, p, RIM : RIM + F]
+    for p in range(PAIRS):
+        enc[:, p * 2 * HD : (p + 1) * 2 * HD] = wide[tok, p, RIM : RIM + F]
+    copies = [pltpu.make_async_copy(enc, enc_hbm, sem.at[0])]
+    copies[0].start()
     left = lax.broadcasted_iota(jnp.int32, (1, 2 * DHD), 1) < DHD
     for p in range(queries.shape[1] // (2 * DHD)):
         cols = slice(p * 2 * DHD, (p + 1) * 2 * DHD)
@@ -495,14 +543,18 @@
             top = jnp.max(scores, axis=1, keepdims=True)
             raised = jnp.exp((scores - top) * DHD ** (-0.5))
             whole = 1.0 / jnp.sum(raised, axis=1, keepdims=True)
-            both.append(dot((raised * whole).astype(BF), v_pair))
-        out_ref[:, cols] = jnp.where(left, both[0], both[1]).astype(BF)
+            both.append(dot(raised.astype(BF), v_pair) * whole)
+        out[:, cols] = jnp.where(left, both[0], both[1]).astype(BF)
+        copies.append(pltpu.make_async_copy(out.at[:, cols], out_hbm.at[:, cols], sem.at[p + 1]))
+        copies[-1].start()
+    for copy in copies:
+        copy.wait()
 
 
 def solution(mesh):
     frames = mesh.shape["frames"]
     tok_count = mesh.shape["tok"]
-    ng = min(4, frames // NI)
+    ng = min(16 // NI, frames // NI)
     ny = frames // (NI * ng)
     sub = PIECE // ng
     vmem = pl.BlockSpec(memory_space=pltpu.VMEM)
@@ -516,7 +568,7 @@
         wide, keys, values, held, bias = pl.pallas_call(
             functools.partial(mixer, (ny, ng, tok_count)),
             out_shape=(
-                jax.ShapeDtypeStruct((tok_count, NI, window, PIECE), BF),
+                jax.ShapeDtypeStruct((tok_count, PAIRS, window, N), BF),
                 jax.ShapeDtypeStruct((window, out_width), BF),
                 jax.ShapeDtypeStruct((window, out_width), BF),
                 jax.ShapeDtypeStruct(queries.shape, BF),
@@ -548,16 +600,16 @@
                 pltpu.VMEM((ny, 8, N), F32),
                 pltpu.VMEM((2, ng, sub, N), BF),
                 pltpu.VMEM((2, ng, sub, N), BF),
-                pltpu.VMEM((NI, count, PIECE), F32),
-                pltpu.VMEM((NI, count, PIECE), BF),
-                pltpu.VMEM((NI, RIM, PIECE), BF),
-                pltpu.VMEM((NI, RIM, PIECE), BF),
+                pltpu.VMEM((PAIRS, count, N), F32),
+                pltpu.VMEM((PAIRS, count, N), BF),
+                pltpu.VMEM((PAIRS, RIM, N), BF),
+                pltpu.VMEM((PAIRS, RIM, N), BF),
                 pltpu.VMEM((2, NI, PIECE, N), BF),
-                pltpu.VMEM((2, NI, count, PIECE), F32),
-                pltpu.VMEM((NI, count, PIECE), F32),
-                pltpu.VMEM((2 * RIM + NI * count, PIECE), BF),
-                pltpu.VMEM((NI, window, PIECE), BF),
-                pltpu.VMEM((NI, RIM, PIECE), BF),
+                pltpu.VMEM((2, NI, LP, count, N), F32),
+                pltpu.VMEM((NI, LP, count, N), F32),
+                pltpu.VMEM((LP, 2 * RIM + NI * count, N), BF),
+                pltpu.VMEM((PAIRS, window, N), BF),
+                pltpu.VMEM((PAIRS, RIM, N), BF),
                 pltpu.VMEM((window, out_width), F32),
                 pltpu.VMEM((window, out_width), F32),
                 pltpu.SemaphoreType.DMA((10,)),
@@ -591,7 +643,12 @@
                 jax.ShapeDtypeStruct(queries.shape, BF),
             ),
             in_specs=[vmem] * 5,
-            out_specs=(vmem, vmem),
+            out_specs=(hbm, hbm),
+            scratch_shapes=[
+                pltpu.VMEM((count, width), BF),
+                pltpu.VMEM(queries.shape, BF),
+                pltpu.SemaphoreType.DMA((out_width // (2 * DHD) + 1,)),
+            ],
             compiler_params=pltpu.CompilerParams(vmem_limit_bytes=24 * 2**20),
         )(wide, keys, values, held, bias)
 

time: 60.1 us -> 58 us (0.965)
  Pallas kernels: 59.3 us -> 57.3 us
    pallas_call x1, Pallas kernels: 56.8 us -> 55.2 us  [local(): pl.pallas_call(functools.partial(mixer, (ny, ng, tok_count)), out_shape=(...]
where the time goes in v2:
time: 58 us; the launch traced here: 57.9 us
  Pallas kernels  57.3 us (99%)
  between operations  0.64 us (1%)
    pallas_call x1, Pallas kernels, local(): pl.pallas_call(functools.partial(mixer, (ny, ng, tok_count)), out_shape=(...  55.2 us
    pallas_call x1, Pallas kernels, local(): pl.pallas_call(reader, out_shape=(jax.ShapeDtypeStruct((count, width), BF...  2.02 us

profile of v2, /device:TPU:1, one launch (start us, length us, event | category | flops | bytes accessed | tf_op | source)
XLA Modules:
  0.0 57.9 jit_solution(7657597050001206677)
XLA Ops:
  0.6 55.2 %shard_map.113 = (bf16[2,4,256,128]{3,2,1,0:T(8,128)(2,1)S(1)}, bf16[256,640]{1,0:T(8,128)(2,1)S(1)}, bf16[256,640]{1,0:T(8,128)(2,1)S(1)}, bf16[256,640]{1,0:T(8,128)(2,1)S(1)}, f32[256,256]{1,0:T(8,128)S(1)}) custom-call(bf16[128,512]{1,0:T(8,128)(2,1)} %x_hbm.1, bf16[128,128]{1,0:T(8,128)(2,1)} %b_hbm.1, bf16[128,128]{1,0:T(8,128)(2,1)} %c_hbm.1, ...), custom_call_target="tpu_custom_call" | custom-call | tf_op jit(solution)/shard_map/pallas_call | solution.py:568
  55.9 2.0 %shard_map.114 = (bf16[128,512]{1,0:T(8,128)(2,1)}, bf16[256,640]{1,0:T(8,128)(2,1)}) custom-call(bf16[2,4,256,128]{3,2,1,0:T(8,128)(2,1)S(1)} %get-tuple-element.7.wide, bf16[256,640]{1,0:T(8,128)(2,1)S(1)} %get-tuple-element.8.keys, bf16[256,640]{1,0:T(8,128)(2,1)S(1)} %get-tuple-element.9.values, bf16[256,640]{1,0:T(8,128)(2,1)S(1)} %get-tuple-element.10.queries, ...), custom_call_target="tpu_custom_call" | custom-call | tf_op jit(solution)/shard_map/pallas_call | solution.py:639
